TPU v7x, 32 devices: a whole 2x2x4 slice. The times are simulated.
32 devices in a mesh: groups: 2 (over x), tensor: 8 (over z, y), dp: 2 (over core).
Axes of the slice: x: 2, y: 2, z: 4, core: 2. Of those that a mesh axis runs over, the one named last changes fastest.
Arguments:
- tokens: bfloat16 [2048, 8192], P(('groups', 'dp'), 'tensor'), parts along dimension 0, may hold values from -6 to 6
- cotangent: bfloat16 [2048, 8192], P(('groups', 'dp'), 'tensor'), parts along dimension 0, may hold values from -6 to 6
- up_weight: bfloat16 [8192, 28672], P('dp', 'tensor'), may hold values from -0.0625 to 0.0625
- down_weight: bfloat16 [28672, 8192], P('tensor', 'dp'), may hold values from -0.03125 to 0.03125
- proj_inputs: bfloat16 [8192, 64], P('tensor'), may hold values from -0.0625 to 0.0625
- proj_hidden: bfloat16 [28672, 64], P('tensor'), may hold values from -0.03125 to 0.03125
- proj_hgrad: bfloat16 [28672, 64], P('tensor'), may hold values from -0.03125 to 0.03125
- proj_outgrad: bfloat16 [8192, 64], P('tensor'), may hold values from -0.0625 to 0.0625
- segment_ids: int32 [2048], P(('groups', 'dp')), parts along dimension 0, may hold values from 0 to 7, never falling along the last dimension, each value on 1 to 384 neighbouring positions
- queries: bfloat16 [512, 8192], P(('tensor', 'dp')), may hold values from -0.015625 to 0.015625
Outputs:
- scores: float32 [16, 512], P(('groups', 'dp'), 'tensor'), parts along dimension 0
There are 2 independent parts, one for each index of `groups`. A program takes and returns all parts, laid end to end along the dimension named above; an argument that names none is the same for every part. Nothing has to cross between parts.
Inputs may be any that keep to these rules, and one draw needn't show every extreme that they name: `segment_ids`: Non-decreasing along the window; each of the 8 examples has 1 to 384 tokens and one has exactly 384.
All inputs are finite; a program needn't handle non-finite values.
Results may differ from a plain program's by a relative error of at most 0.0029.
Values may be sent and summed in bfloat16 or wider, within the bound.
A program may use at most 256 MiB of HBM per device.

v0:
```python
import jax
import jax.numpy as jnp
from jax import lax
from jax.sharding import PartitionSpec as P

EX_DEV = 4


def swapped(block, axis, bit):
    count = lax.axis_size(axis)
    route = []
    for low in range(count):
        high = low | 1 << bit
        if high != low and high < count:
            route += [(low, high), (high, low)]
    return lax.ppermute(block, axis, route)


def example_grads(left, right, segment_ids, count, rank):
    onehot = (segment_ids[:, None] == jnp.arange(count, dtype=jnp.int32)[None, :]).astype(
        jnp.float32
    )
    weighted = (onehot[:, :, None] * left[:, None, :]).reshape(left.shape[0], count * rank)
    outer = lax.dot_general(
        weighted,
        right,
        (((0,), (0,)), ((), ())),
        precision=lax.Precision.HIGHEST,
        preferred_element_type=jnp.float32,
    )
    return outer.reshape(count, rank * rank)


def contract_last(left, right):
    return lax.dot_general(
        left, right, (((1,), (1,)), ((), ())), preferred_element_type=jnp.float32
    )


def shards(
    tokens,
    cotangent,
    up_weight,
    down_weight,
    proj_inputs,
    proj_hidden,
    proj_hgrad,
    proj_outgrad,
    segment_ids,
    queries,
):
    rank = proj_inputs.shape[1]
    part_in = jnp.dot(tokens, proj_inputs, preferred_element_type=jnp.float32)
    part_out = jnp.dot(cotangent, proj_outgrad, preferred_element_type=jnp.float32)
    full_x, full_dy = (
        lax.all_gather(tokens, "tensor", axis=1, tiled=True),
        lax.all_gather(cotangent, "tensor", axis=1, tiled=True),
    )
    half = up_weight.shape[0]
    side = lax.axis_index("dp")
    own_x = lax.dynamic_slice_in_dim(full_x, side * half, half, 1)
    own_dy = lax.dynamic_slice_in_dim(full_dy, side * half, half, 1)
    far_x = lax.dynamic_slice_in_dim(full_x, (1 - side) * half, half, 1)
    far_dy = lax.dynamic_slice_in_dim(full_dy, (1 - side) * half, half, 1)
    recv_x, recv_dy = swapped((far_x, far_dy), "dp", 0)
    lent_pre = jnp.dot(recv_x, up_weight, preferred_element_type=jnp.float32)
    lent_back = contract_last(recv_dy, down_weight)
    ret_pre, ret_back = swapped((lent_pre, lent_back), "dp", 0)
    pre = jnp.dot(own_x, up_weight, preferred_element_type=jnp.float32) + ret_pre
    back = contract_last(own_dy, down_weight) + ret_back
    hidden = jax.nn.silu(pre).astype(jnp.bfloat16)
    sig = jax.nn.sigmoid(pre)
    hgrad = (back * sig * (1.0 + pre * (1.0 - sig))).astype(jnp.bfloat16)
    part_hg = jnp.dot(hgrad, proj_hgrad, preferred_element_type=jnp.float32)
    part_hid = jnp.dot(hidden, proj_hidden, preferred_element_type=jnp.float32)
    stacked = jnp.concatenate([part_in, part_hg, part_hid, part_out], axis=1)
    factors = lax.psum(stacked, "tensor")
    count = 2 * (segment_ids.shape[0] * 0 + queries.shape[0] * 0) + 0
    count = EX_DEV * 2
    grads = jnp.concatenate(
        [
            example_grads(factors[:, :rank], factors[:, rank : 2 * rank], segment_ids, count, rank),
            example_grads(
                factors[:, 2 * rank : 3 * rank], factors[:, 3 * rank :], segment_ids, count, rank
            ),
        ],
        axis=1,
    )
    block = lax.all_gather(queries, "dp", axis=0, tiled=True).astype(jnp.float32)
    mine = lax.psum_scatter(grads, "dp", scatter_dimension=0, tiled=True)
    scores = lax.dot_general(
        mine,
        block,
        (((1,), (1,)), ((), ())),
        precision=lax.Precision.HIGHEST,
        preferred_element_type=jnp.float32,
    )
    return scores


def solution(mesh):
    placed = (
        P(("groups", "dp"), "tensor"),
        P(("groups", "dp"), "tensor"),
        P("dp", "tensor"),
        P("tensor", "dp"),
        P("tensor", None),
        P("tensor", None),
        P("tensor", None),
        P("tensor", None),
        P(("groups", "dp")),
        P(("tensor", "dp"), None),
    )
    return jax.shard_map(
        shards, mesh=mesh, in_specs=placed, out_specs=P(("groups", "dp"), "tensor"), check_vma=False
    )
```

profile of v0, /device:TPU:0, one launch (start us, length us, event | category | flops | bytes accessed | tf_op | source)
XLA Modules:
  0.0 476.5 jit_solution(5143397714507449067)
XLA Ops:
  7.4 0.0 copy-start
  7.4 0.0 all-gather.6.cloned.1.call-start
  7.4 0.7 all-gather.6.cloned.1.call-update
  8.1 0.0 all-gather.4.cloned.1.call-start
  8.1 0.7 all-gather.4.cloned.1.call-update
  8.8 0.0 all-reduce.4.cloned.1.call-start
  8.9 129.1 %all-gather.6.cloned.1.call-done = bf16[512,8192]{1,0:T(8,128)(2,1)} async-done(((bf16[512,1024]{1,0:T(8,128)(2,1)}), bf16[512,8192]{1,0:T(8,128)(2,1)}) %all-gather.6.cloned.1.call-update) | async-done | bytes 8388624 | tf_op jit(solution)/shard_map/all_gather | solution.py:56
  138.0 4.7 constant_dynamic-slice_fusion
  142.7 0.0 collective-permute-start.2
  142.7 120.6 %all-gather.4.cloned.1.call-done = bf16[512,8192]{1,0:T(8,128)(2,1)} async-done(((bf16[512,1024]{1,0:T(8,128)(2,1)}), bf16[512,8192]{1,0:T(8,128)(2,1)}) %all-gather.4.cloned.1.call-update) | async-done | bytes 8388624 | tf_op jit(solution)/shard_map/all_gather | solution.py:57
  263.3 2.5 constant_dynamic-slice_fusion.1
  265.8 0.1 collective-permute-start
  265.9 0.0 collective-permute-done.2
  265.9 24.0 %fusion.28 = f32[512,3584]{1,0:T(8,128)} fusion(bf16[512,4096]{1,0:T(8,128)(2,1)} %collective-permute-done.2, bf16[4096,3584]{1,0:T(8,128)(2,1)} %param.12), kind=kOutput, calls=%fused_computation.33 | convolution fusion | flops 15032385536 | bytes 40894464 | tf_op jit(solution)/shard_map/dot_general | solution.py:66
  289.9 0.0 copy-start.1
  289.9 0.0 copy-start.3
  289.9 0.0 copy-start.2
  289.9 0.0 copy-start.4
  289.9 0.5 collective-permute-start.3
  290.4 0.0 collective-permute-done
  290.4 23.5 %fusion.27 = f32[512,3584]{1,0:T(8,128)} fusion(bf16[512,4096]{1,0:T(8,128)(2,1)} %collective-permute-done, bf16[3584,4096]{1,0:T(8,128)(2,1)} %param.13), kind=kOutput, calls=%fused_computation.32 | convolution fusion | flops 15032385536 | bytes 40894464 | tf_op jit(solution)/shard_map/dot_general | solution.py:35
  314.0 0.0 collective-permute-start.1
  314.0 0.0 copy-done.1
  314.0 0.0 copy-done.3
  314.0 0.4 fusion.26
  314.5 0.0 copy-done.2
  314.5 0.0 copy-done.4
  314.5 0.4 fusion.29
  314.9 24.1 %fusion = f32[512,3584]{1,0:T(8,128)} fusion(bf16[4096,3584]{1,0:T(8,128)(2,1)} %param.12, bf16[512,8192]{1,0:T(8,128)(2,1)} %all-gather.6.cloned.1.call-done, s32[]{:T(128)S(6)} %select_n.8), kind=kOutput, calls=%fused_computation.3 | convolution fusion | flops 15032385536 | bytes 40894468 | tf_op jit(solution)/shard_map/dot_general | solution.py:69
  339.0 0.0 copy-start.6
  339.0 0.0 collective-permute-done.3
  339.0 0.0 copy-done
  339.0 6.4 %fusion.4 = f32[512,64]{0,1:T(8,128)S(1)} fusion(bf16[3584,64]{0,1:T(8,128)(2,1)S(1)} %copy-done, f32[512,3584]{1,0:T(8,128)} %fusion, f32[512,3584]{1,0:T(8,128)} %collective-permute-done.3), kind=kOutput, calls=%fused_computation.7 | convolution fusion | flops 245891072 | bytes 15269888 | tf_op jit(solution)/shard_map/dot_general | solution.py:75
  345.5 0.0 copy-start.5
  345.5 0.0 collective-permute-done.1
  345.5 0.0 copy-done.6
  345.5 26.1 %fusion.5 = f32[512,64]{0,1:T(8,128)S(1)} fusion(bf16[3584,64]{0,1:T(8,128)(2,1)S(1)} %copy-done.6, f32[512,3584]{1,0:T(8,128)} %collective-permute-done.1, bf16[3584,4096]{1,0:T(8,128)(2,1)} %param.13, bf16[512,8192]{1,0:T(8,128)(2,1)} %all-gather.4.cloned.1.call-done, s32[]{:T(128)S(6)} %select_n.8, f32[512,3584]{1,0:T(8,128)} %fusion, ...), kind=kOutput, calls=%fused_computation.8 | convolution fusion | flops 15287451648 | bytes 56164356 | tf_op jit(solution)/shard_map/dot_general | solution.py:74
  371.6 0.0 copy-start.7
  371.6 0.8 pad_maximum_fusion
  372.5 0.0 all-reduce.4.cloned.1.call-update
  372.5 0.0 all-gather.8.cloned.1.call-start
  372.5 0.5 all-gather.8.cloned.1.call-update
  373.1 0.3 all-reduce.6.cloned.1.call-start
  373.3 0.0 copy-done.5
  373.4 69.9 %all-reduce.4.cloned.1.call-done = f32[512,256]{0,1:T(8,128)} async-done(((f32[512,256]{0,1:T(8,128)}), f32[512,256]{0,1:T(8,128)}) %all-reduce.4.cloned.1.call-update) | async-done | bytes 524304 | tf_op jit(solution)/shard_map/psum | solution.py:77
  443.3 1.0 fusion.25
  444.2 0.3 broadcast_multiply_fusion.1
  444.5 1.9 fusion.14
  446.4 0.1 reshape.38
  446.5 1.9 fusion.12
  448.4 0.1 reshape.39
  448.5 0.7 pad_maximum_fusion.1
  449.2 0.0 all-reduce.6.cloned.1.call-update
  449.2 0.0 copy-done.7
  449.2 0.6 dynamic-slice
  450.5 0.0 all-gather.8.cloned.1.call-done
  450.5 16.0 %all-reduce.6.cloned.1.call-done = f32[8,8192]{1,0:T(8,128)} async-done(((f32[8,8192]{1,0:T(8,128)}), f32[8,8192]{1,0:T(8,128)}) %all-reduce.6.cloned.1.call-update) | async-done | bytes 262160
  466.5 2.8 fusion.16
  (1 shorter events, 0.0 us)
Async XLA Ops:
  7.4 331.7 %copy-start = (bf16[3584,64]{0,1:T(8,128)(2,1)S(1)}, bf16[3584,64]{0,1:T(8,128)(2,1)}, u32[]{:S(2)}) copy-start(bf16[3584,64]{0,1:T(8,128)(2,1)} %param.15) | copy-start | bytes 1376260
  7.4 130.7 %all-gather.6.cloned.1.call-start = ((), (), s32[]{:S(2)}) async-start(), calls=%async_computation.1 | async-start | bytes 9437184 | tf_op jit(solution)/shard_map/all_gather | solution.py:56
  8.1 255.3 %all-gather.4.cloned.1.call-start = ((), (), s32[]{:S(2)}) async-start(), calls=%async_computation | async-start | bytes 9437184 | tf_op jit(solution)/shard_map/all_gather | solution.py:57
  8.8 434.4 %all-reduce.4.cloned.1.call-start = ((), (), s32[]{:S(2)}) async-start(), calls=%async_computation.2 | async-start | bytes 1048576 | tf_op jit(solution)/shard_map/psum | solution.py:77
  142.7 123.2 %collective-permute-start.2 = (bf16[512,4096]{1,0:T(8,128)(2,1)}, bf16[512,4096]{1,0:T(8,128)(2,1)}, u32[]{:S(2)}, u32[]{:S(2)}) collective-permute-start(bf16[512,4096]{1,0:T(8,128)(2,1)} %constant_dynamic-slice_fusion), channel_id=1, source_target_pairs={{0,1},{1,0},{2,3},{3,2},{4,5},{5,4},{6,7},{7,6},{8,9},{9,8},{10,11... | collective-permute-start | bytes 12582920 | tf_op jit(solution)/shard_map/ppermute | solution.py:16
  265.8 24.6 %collective-permute-start = (bf16[512,4096]{1,0:T(8,128)(2,1)S(1)}, bf16[512,4096]{1,0:T(8,128)(2,1)}, u32[]{:S(2)}, u32[]{:S(2)}) collective-permute-start(bf16[512,4096]{1,0:T(8,128)(2,1)S(1)} %constant_dynamic-slice_fusion.1), channel_id=1, source_target_pairs={{0,1},{1,0},{2,3},{3,2},{4,5},{5,4},{6,7},{7,6},{8,9},{9,8},{10,11... | collective-permute-start | bytes 12582920 | tf_op jit(solution)/shard_map/ppermute | solution.py:16
  289.9 24.1 %copy-start.1 = (bf16[512,1024]{1,0:T(8,128)(2,1)S(1)}, bf16[512,1024]{1,0:T(8,128)(2,1)}, u32[]{:S(2)}) copy-start(bf16[512,1024]{1,0:T(8,128)(2,1)} %param.10) | copy-start | bytes 3145732
  289.9 24.1 %copy-start.3 = (bf16[1024,64]{0,1:T(8,128)(2,1)S(1)}, bf16[1024,64]{0,1:T(8,128)(2,1)}, u32[]{:S(2)}) copy-start(bf16[1024,64]{0,1:T(8,128)(2,1)} %param.14) | copy-start | bytes 393220
  289.9 24.6 %copy-start.2 = (bf16[512,1024]{1,0:T(8,128)(2,1)S(1)}, bf16[512,1024]{1,0:T(8,128)(2,1)}, u32[]{:S(2)}) copy-start(bf16[512,1024]{1,0:T(8,128)(2,1)} %param.11) | copy-start | bytes 3145732
  289.9 24.6 %copy-start.4 = (bf16[1024,64]{0,1:T(8,128)(2,1)S(1)}, bf16[1024,64]{0,1:T(8,128)(2,1)}, u32[]{:S(2)}) copy-start(bf16[1024,64]{0,1:T(8,128)(2,1)} %param.17) | copy-start | bytes 393220
  289.9 49.1 %collective-permute-start.3 = (f32[512,3584]{1,0:T(8,128)}, f32[512,3584]{1,0:T(8,128)}, u32[]{:S(2)}, u32[]{:S(2)}) collective-permute-start(f32[512,3584]{1,0:T(8,128)} %fusion.28), channel_id=1, source_target_pairs={{0,1},{1,0},{2,3},{3,2},{4,5},{5,4},{6,7},{7,6},{8,9},{9,8},{10,11... | collective-permute-start | bytes 22020104 | tf_op jit(solution)/shard_map/ppermute | solution.py:16
  314.0 31.5 %collective-permute-start.1 = (f32[512,3584]{1,0:T(8,128)}, f32[512,3584]{1,0:T(8,128)}, u32[]{:S(2)}, u32[]{:S(2)}) collective-permute-start(f32[512,3584]{1,0:T(8,128)} %fusion.27), channel_id=1, source_target_pairs={{0,1},{1,0},{2,3},{3,2},{4,5},{5,4},{6,7},{7,6},{8,9},{9,8},{10,11... | collective-permute-start | bytes 22020104 | tf_op jit(solution)/shard_map/ppermute | solution.py:16
  339.0 6.5 %copy-start.6 = (bf16[3584,64]{0,1:T(8,128)(2,1)S(1)}, bf16[3584,64]{0,1:T(8,128)(2,1)}, u32[]{:S(2)}) copy-start(bf16[3584,64]{0,1:T(8,128)(2,1)} %param.16) | copy-start | bytes 1376260
  345.5 27.9 %copy-start.5 = (s32[512]{0:T(512)S(1)}, s32[512]{0:T(512)}, u32[]{:S(2)}) copy-start(s32[512]{0:T(512)} %param.18) | copy-start | bytes 6148
  371.6 77.6 %copy-start.7 = (u32[32]{0:T(128)S(1)}, u32[32]{0:T(128)}, u32[]{:S(2)}) copy-start(u32[32]{0:T(128)} %constant.18) | copy-start | bytes 388
  372.5 78.0 %all-gather.8.cloned.1.call-start = ((), (), s32[]{:S(2)}) async-start(), calls=%async_computation.3 | async-start | bytes 1572864 | tf_op jit(solution)/shard_map/all_gather | solution.py:89
  373.1 93.5 %all-reduce.6.cloned.1.call-start = ((), (), s32[]{:S(2)}) async-start(), calls=%async_computation.4 | async-start | bytes 524288
Sparse Core Ops, SparseCore 0:
  10.4 127.6 all-gather.5
  140.2 123.0 all-gather.3
  372.6 70.5 all-reduce.3
Sparse Core Ops, SparseCore 1:
  374.5 7.1 all-gather.7
  449.3 17.2 all-reduce.5
where the time goes:
time: 477 us; the launch traced here: 476 us
  waiting for transfers between devices  338 us (71%)
  matrix products  112 us (23%)
  between operations  15.4 us (3%)
  local copies, waits for them, and re-layouts  8.99 us (2%)
    all_gather x1, waiting for transfers between devices, shards(): lax.all_gather(tokens, 'tensor', axis=1, tiled=True)  129 us
    all_gather x1, waiting for transfers between devices, shards(): lax.all_gather(cotangent, 'tensor', axis=1, tiled=True)  121 us
    psum x1, waiting for transfers between devices, shards(): factors = lax.psum(stacked, 'tensor')  69.9 us
    dot_general x1, matrix products, shards(): part_hg = jnp.dot(hgrad, proj_hgrad, preferred_element_type=jnp.float32)  26.1 us
    dot_general x1, matrix products, shards(): jnp.dot(own_x, up_weight, preferred_element_type=jnp.float32) + ret_pre  24.1 us
    dot_general x1, matrix products, shards(): lent_pre = jnp.dot(recv_x, up_weight, preferred_element_type=jnp.float32)  24 us
    dot_general x1, matrix products, contract_last(): lax.dot_general(left, right, (((1,), (1,)), ((), ())), preferred_element_...  23.5 us
    unnamed x6, waiting for transfers between devices  18 us
  transfers between devices with their start and end apart: 9, of which 4 were waited for; matrix products, arithmetic and copies ran while one was open for 19% of the time, Pallas kernels for 0%

commit v1 on v0

--- a/solution.py
+++ b/solution.py
@@ -1,9 +1,17 @@
+import functools
+
 import jax
 import jax.numpy as jnp
 from jax import lax
+from jax.experimental import pallas as pl
+from jax.experimental.pallas import tpu as pltpu
 from jax.sharding import PartitionSpec as P
 
+MESH = pl.DeviceIdType.MESH
+F32 = jnp.float32
+BF16 = jnp.bfloat16
 EX_DEV = 4
+TILE = 512
 
 
 def swapped(block, axis, bit):
@@ -37,7 +45,7 @@
     )
 
 
-def shards(
+def general(
     tokens,
     cotangent,
     up_weight,
@@ -75,7 +83,6 @@
     part_hid = jnp.dot(hidden, proj_hidden, preferred_element_type=jnp.float32)
     stacked = jnp.concatenate([part_in, part_hg, part_hid, part_out], axis=1)
     factors = lax.psum(stacked, "tensor")
-    count = 2 * (segment_ids.shape[0] * 0 + queries.shape[0] * 0) + 0
     count = EX_DEV * 2
     grads = jnp.concatenate(
         [
@@ -96,6 +103,343 @@
         preferred_element_type=jnp.float32,
     )
     return scores
+
+
+def units(*names):
+    return [(int(u[0]), 1 if u.endswith("'") else 0, "xd".index(u[1])) for u in names]
+
+
+END = units("0x", "0d", "1x", "0x'", "1d", "0d'", "2x", "1x'", "2d", "1d'", "3x", "2x'", "3d", "2d'", "3x'", "3d'")
+MID = units("1x", "1d", "2x", "0x", "2d", "0d", "1x'", "3x", "1d'", "3d", "2x'", "0x'", "2d'", "0d'", "3x'", "3d'")
+END_NEAR = units("0x", "0d", "1x", "0x'", "1d", "0d'", "1x'", "1d'")
+MID_NEAR = units("1x", "1d", "0x", "1x'", "0d", "1d'", "0x'", "0d'")
+FAR = units("2x", "2d", "3x", "2x'", "3d", "2d'", "3x'", "3d'")
+END_TO = {"0x": (0, 2), "0d": (0, 2), "1x": (2,), "1d": (2,), "2x": (2,), "2d": (2,), "3x": (2,), "0x'": (0,), "0d'": (0,)}
+MID_TO = {"1x": (0, 1, 2), "1d": (0, 1, 2), "2x": (0, 2), "2d": (0, 2), "3x": (0, 2), "3d": (0, 2), "0x": (1,), "0d": (1,), "3d'": (0,)}
+END_SENDS = {units(u)[0]: to for u, to in END_TO.items()}
+MID_SENDS = {units(u)[0]: to for u, to in MID_TO.items()}
+
+
+def kernel(
+    tok, cot, up, down, pin, phid, phg, pout, qry,
+    in_up, out_up, in_down, out_down, up_far, down_far, q_far,
+    held, pre, back, wbuf, part, land, full,
+    own_sem, w_sem, send_sem, recv_sem, hs_sem, hr_sem, ws_sem, wr_sem, fs_sem, fr_sem,
+):
+    rows, feats = tok.shape
+    tiles = pre.shape[0]
+    n = full.shape[1]
+    me = lax.axis_index("tensor")
+    d = lax.axis_index("dp")
+    z, y = me // 2, me % 2
+    s = z // 2
+    is_end = (z == 0) | (z == 3)
+    is_mid = jnp.logical_not(is_end)
+
+    def place(m):
+        return m + s * (3 - 2 * m)
+
+    def source(unit):
+        m, row, _ = unit
+        return place(m) * 2 + (y if row == 0 else 1 - y)
+
+    def either(a, b):
+        return jnp.where(is_end, a, b)
+
+    nbr = (either(place(1), place(0)) * 2 + y, place(2) * 2 + y, z * 2 + 1 - y)
+
+    barrier = pltpu.get_barrier_semaphore()
+    for k in range(1, n):
+        pl.semaphore_signal(barrier, inc=1, device_id={"tensor": lax.rem(me + k, n)}, device_id_type=MESH)
+    pl.semaphore_signal(barrier, inc=1, device_id={"dp": 1 - d}, device_id_type=MESH)
+
+    mine = [
+        pltpu.make_async_copy(tok, held.at[me * 2], own_sem.at[0]),
+        pltpu.make_async_copy(cot, held.at[me * 2 + 1], own_sem.at[1]),
+    ]
+    for c in mine:
+        c.start()
+    pl.semaphore_wait(barrier, n)
+
+    def in_halves(link, unit):
+        return unit[0] == 3 and (link == 2 or unit[1] == 1)
+
+    def send_half(link, unit, h):
+        slot = source(unit) * 2 + unit[2]
+        part_of = pl.ds(h * (rows // 2), rows // 2)
+        return pltpu.make_async_remote_copy(
+            src_ref=held.at[slot, part_of], dst_ref=held.at[slot, part_of],
+            send_sem=hs_sem.at[unit[2], unit[1], h], recv_sem=hr_sem.at[unit[2], h],
+            device_id={"tensor": nbr[link]}, device_id_type=MESH,
+        )
+
+    def send(link, unit):
+        slot = source(unit) * 2 + unit[2]
+        return pltpu.make_async_remote_copy(
+            src_ref=held.at[slot], dst_ref=held.at[slot],
+            send_sem=send_sem.at[link, slot], recv_sem=recv_sem.at[slot],
+            device_id={"tensor": nbr[link]}, device_id_type=MESH,
+        )
+
+    def copies(link, unit):
+        if in_halves(link, unit):
+            return [send_half(link, unit, h) for h in range(2)]
+        return [send(link, unit)]
+
+    def forward(step):
+        for role, order, sends in ((is_end, END, END_SENDS), (is_mid, MID, MID_SENDS)):
+            links = sends.get(order[step], ())
+            if links:
+                @pl.when(role)
+                def _():
+                    for link in links:
+                        for c in copies(link, order[step]):
+                            c.start()
+
+    def slot_of(step):
+        return either(source(END[step]), source(MID[step])) * 2 + END[step][2]
+
+    def block(near, far, kind, src):
+        at = pl.ds(pl.multiple_of((src % 4) * feats, feats), feats)
+        return (near.at[at], far.at[at]) if kind == 0 else (near.at[:, at], far.at[:, at])
+
+    def lend(kind, src):
+        here, there = block(up, up_far, 0, src) if kind == 0 else block(down, down_far, 1, src)
+        return pltpu.make_async_remote_copy(
+            src_ref=here, dst_ref=there,
+            send_sem=ws_sem.at[kind, src % 4], recv_sem=wr_sem.at[kind, src % 4],
+            device_id={"dp": 1 - d}, device_id_type=MESH,
+        )
+
+    lent = []
+    for k in range(8):
+        near = either(source(END_NEAR[k]), source(MID_NEAR[k]))
+        lent.append((FAR[k][2], jnp.where(s == d, near, source(FAR[k]))))
+
+    q_copy = pltpu.make_async_remote_copy(
+        src_ref=qry, dst_ref=q_far, send_sem=own_sem.at[2], recv_sem=own_sem.at[3],
+        device_id={"dp": 1 - d}, device_id_type=MESH,
+    )
+
+    for step in range(2):
+        mine[step].wait()
+        forward(step)
+    for kind, src in lent:
+        lend(kind, src).start()
+    q_copy.start()
+
+    def load(step):
+        kind, b = END[step][2], step % 2
+        src = slot_of(step) // 2
+
+        def tiles_from(w):
+            at = pl.multiple_of((src % 4) * feats, feats)
+
+            def body(i, carry):
+                cols = pl.ds(pl.multiple_of(i * TILE, TILE), TILE)
+                if kind == 0:
+                    pltpu.make_async_copy(w.at[pl.ds(at, feats), cols], wbuf.at[b, i], w_sem.at[b]).start()
+                else:
+                    for h in range(feats // TILE):
+                        pltpu.make_async_copy(
+                            w.at[cols, pl.ds(at + h * TILE, TILE)],
+                            wbuf.at[b, i, pl.ds(h * TILE, TILE)], w_sem.at[b],
+                        ).start()
+                return carry
+
+            lax.fori_loop(0, tiles, body, 0)
+
+        @pl.when(src // 4 == d)
+        def _():
+            tiles_from((up, down)[kind])
+
+        @pl.when(src // 4 != d)
+        def _():
+            lend(kind, src).wait_recv()
+            tiles_from((up_far, down_far)[kind])
+
+    def product(kind, slot, b, i, at=slice(None)):
+        a = held[slot, at]
+        if kind == 0:
+            return jnp.dot(a, wbuf[b, i], preferred_element_type=F32)
+        out = None
+        for h in range(feats // TILE):
+            p = lax.dot_general(
+                a[:, h * TILE:(h + 1) * TILE], wbuf[b, i, h * TILE:(h + 1) * TILE],
+                (((1,), (1,)), ((), ())), preferred_element_type=F32,
+            )
+            out = p if out is None else out + p
+        return out
+
+    def peer_copy(g, phase, k):
+        peer = lax.rem(me + k, n)
+        src, dst = (part.at[g, peer], land.at[g, me]) if phase == 0 else (full.at[g, me], full.at[g, me])
+        return pltpu.make_async_remote_copy(
+            src_ref=src, dst_ref=dst, send_sem=fs_sem.at[g, phase, peer], recv_sem=fr_sem.at[g, phase, me],
+            device_id={"tensor": peer}, device_id_type=MESH,
+        )
+
+    def arrived(g, phase, k):
+        peer = lax.rem(me + k, n)
+        ref = land.at[g, peer] if phase == 0 else full.at[g, peer]
+        pltpu.make_async_remote_copy(
+            src_ref=ref, dst_ref=ref, send_sem=fs_sem.at[g, phase, peer], recv_sem=fr_sem.at[g, phase, peer],
+            device_id={"tensor": peer}, device_id_type=MESH,
+        ).wait_recv()
+
+    def start_all(g, phase):
+        for k in range(1, n):
+            peer_copy(g, phase, k).start()
+
+    def add_up(g):
+        total = part[g, me]
+        for k in range(1, n):
+            arrived(g, 0, k)
+            total = total + land[g, lax.rem(me + k, n)]
+        full[g, me] = total
+        start_all(g, 1)
+
+    def keep(g, col, value, first=0):
+        r = rows // n
+        w = value.shape[1]
+        for k in range(value.shape[0] // r):
+            part[g, first + k, :, col * w:(col + 1) * w] = value[k * r:(k + 1) * r]
+
+    load(0)
+    for step in range(14):
+        kind, b = END[step][2], step % 2
+        slot = slot_of(step)
+        if step >= 2:
+            pltpu.make_async_copy(held.at[slot], held.at[slot], recv_sem.at[slot]).wait()
+            forward(step)
+        pltpu.make_async_copy(wbuf.at[b], wbuf.at[b], w_sem.at[b]).wait()
+        load(step + 1)
+        acc = (pre, back)[kind]
+        if step == 0:
+            keep(0, 0, contract_last(held[slot], pin[...]))
+        if step == 1:
+            keep(0, 1, contract_last(held[slot], pout[...]))
+            start_all(0, 0)
+        if step == 8:
+            add_up(0)
+        if step < 2:
+            def body(i, carry):
+                acc[i] = product(kind, slot, b, i)
+                return carry
+            lax.fori_loop(0, tiles, body, 0)
+        else:
+            def body(i, carry):
+                acc[i] += product(kind, slot, b, i)
+                return carry
+            lax.fori_loop(0, tiles, body, 0)
+    load(15)
+    half = rows // 2
+    for h in range(2):
+        at = slice(h * half, (h + 1) * half)
+        for kind in range(2):
+            slot = slot_of(14 + kind)
+            there = held.at[slot, pl.ds(h * half, half)]
+            pltpu.make_async_copy(there, there, hr_sem.at[kind, h]).wait()
+            if kind == 1:
+                @pl.when(is_mid)
+                def _():
+                    send_half(0, MID[15], h).start()
+            if h == 0:
+                pltpu.make_async_copy(wbuf.at[kind], wbuf.at[kind], w_sem.at[kind]).wait()
+            weight = (phid, phg)[kind]
+
+            def body(i, total):
+                cols = pl.ds(pl.multiple_of(i * TILE, TILE), TILE)
+                v = (pre, back)[kind][i, at] + product(kind, slot, kind, i, at)
+                if kind == 0:
+                    sig = jax.nn.sigmoid(v)
+                    pre[i, at] = sig * (1.0 + v * (1.0 - sig))
+                    u = v * sig
+                else:
+                    u = v * pre[i, at]
+                return total + contract_last(u.astype(BF16), weight[:, cols])
+
+            total = lax.fori_loop(0, tiles, body, jnp.zeros((half, weight.shape[0]), F32))
+            keep(1, 1 - kind, total, h * (n // 2))
+    start_all(1, 0)
+    add_up(1)
+    for k in range(1, n):
+        arrived(0, 1, k)
+    rank = in_up.shape[2]
+    in_up[...] = full[0, :, :, :rank]
+    out_down[...] = full[0, :, :, rank:]
+    for k in range(1, n):
+        arrived(1, 1, k)
+    out_up[...] = full[1, :, :, :rank]
+    in_down[...] = full[1, :, :, rank:]
+    for g in range(2):
+        for phase in range(2):
+            for k in range(1, n):
+                peer_copy(g, phase, k).wait_send()
+    for role, sends in ((is_end, END_SENDS), (is_mid, MID_SENDS)):
+        @pl.when(role)
+        def _():
+            for unit, links in sends.items():
+                for link in links:
+                    for c in copies(link, unit):
+                        c.wait_send()
+    for kind, src in lent:
+        lend(kind, src).wait_send()
+    q_copy.wait()
+
+
+def fused(
+    tokens, cotangent, up_weight, down_weight, proj_inputs, proj_hidden, proj_hgrad, proj_outgrad, segment_ids, queries,
+):
+    rows, feats = tokens.shape
+    width = up_weight.shape[1]
+    rank = proj_inputs.shape[1]
+    n = lax.axis_size("tensor")
+    tiles = width // TILE
+    hbm = pl.BlockSpec(memory_space=pl.ANY)
+    vmem = pl.BlockSpec(memory_space=pltpu.VMEM)
+    shape = jax.ShapeDtypeStruct
+    dma = pltpu.SemaphoreType.DMA
+    *factors, _, _, q_far = pl.pallas_call(
+        kernel,
+        out_shape=(
+            *[shape((n, rows // n, rank), F32)] * 4,
+            shape(up_weight.shape, BF16), shape(down_weight.shape, BF16), shape(queries.shape, BF16),
+        ),
+        in_specs=[hbm, hbm, hbm, hbm, vmem, vmem, vmem, vmem, hbm],
+        out_specs=(vmem, vmem, vmem, vmem, hbm, hbm, hbm),
+        scratch_shapes=[
+            pltpu.VMEM((2 * n, rows, feats), BF16),
+            pltpu.VMEM((tiles, rows, TILE), F32),
+            pltpu.VMEM((tiles, rows, TILE), F32),
+            pltpu.VMEM((2, tiles, feats, TILE), BF16),
+            pltpu.VMEM((2, n, rows // n, 2 * rank), F32),
+            pltpu.VMEM((2, n, rows // n, 2 * rank), F32),
+            pltpu.VMEM((2, n, rows // n, 2 * rank), F32),
+            dma((4,)), dma((2,)), dma((3, 2 * n)), dma((2 * n,)), dma((2, 2, 2)), dma((2, 2)),
+            dma((2, 4)), dma((2, 4)), dma((2, 2, n)), dma((2, 2, n)),
+        ],
+        compiler_params=pltpu.CompilerParams(collective_id=0, has_side_effects=True, vmem_limit_bytes=60 << 20),
+    )(
+        tokens, cotangent, up_weight, down_weight, proj_inputs.T,
+        proj_hidden.T, proj_hgrad.T, proj_outgrad.T, queries,
+    )
+    in_up, out_up, in_down, out_down = [f.reshape(rows, rank) for f in factors]
+    grads = jnp.concatenate(
+        [
+            example_grads(in_up, out_up, segment_ids, 2 * EX_DEV, rank),
+            example_grads(in_down, out_down, segment_ids, 2 * EX_DEV, rank),
+        ],
+        axis=1,
+    )
+    d = lax.axis_index("dp")
+    block = jnp.where(d == 0, jnp.concatenate([queries, q_far]), jnp.concatenate([q_far, queries])).astype(F32)
+    scores = lax.dot_general(
+        grads, block, (((1,), (1,)), ((), ())), precision=lax.Precision.HIGHEST, preferred_element_type=F32
+    )
+    far = lax.dynamic_slice_in_dim(scores, (1 - d) * EX_DEV, EX_DEV, 0)
+    own = lax.dynamic_slice_in_dim(scores, d * EX_DEV, EX_DEV, 0)
+    return own + swapped(far, "dp", 0)
 
 
 def solution(mesh):
@@ -111,6 +455,7 @@
         P(("groups", "dp")),
         P(("tensor", "dp"), None),
     )
+    fits = mesh.shape["tensor"] == 8 and mesh.shape["dp"] == 2
     return jax.shard_map(
-        shards, mesh=mesh, in_specs=placed, out_specs=P(("groups", "dp"), "tensor"), check_vma=False
-    )
+        fused if fits else general, mesh=mesh, in_specs=placed, out_specs=P(("groups", "dp"), "tensor"), check_vma=False
+    )

time: 477 us -> 204 us (0.43)
  waiting for transfers between devices: 338 us -> 1.14 us
  Pallas kernels: 0 us -> 196 us
  matrix products: 112 us -> 2.89 us
  between operations: 15.4 us -> 0.15 us
  local copies, waits for them, and re-layouts: 8.99 us -> 2.43 us
    all_gather x3 -> x0, waiting for transfers between devices: 250 us -> none  [the longest x1 129 us: shards(): lax.all_gather(tokens, 'tensor', axis=1, tiled=True)]
    pallas_call x0 -> x1, Pallas kernels: none -> 196 us  [fused(): pl.pallas_call(kernel, out_shape=(*[shape((n, rows // n, rank), F32)] * 4...]
    dot_general x8 -> x1, matrix products: 108 us -> 0.92 us  [fused(): lax.dot_general(grads, block, (((1,), (1,)), ((), ())), precision=lax.Pre...]
    psum x1 -> x0, waiting for transfers between devices: 69.9 us -> none  [shards(): factors = lax.psum(stacked, 'tensor')]
    unnamed x6 -> x0, waiting for transfers between devices: 18 us -> none
    dynamic_slice x2 -> x1, local copies, waits for them, and re-layouts: 7.14 us -> 0.01 us  [fused(): far = lax.dynamic_slice_in_dim(scores, (1 - d) * EX_DEV, EX_DEV, 0)]
  transfers between devices with their start and end apart: 9 -> 1, of which waited for: 4 -> 1; matrix products, arithmetic and copies ran while one was open for 19% -> 0% of each run, Pallas kernels for 0% -> 0%
where the time goes in v1:
time: 204 us; the launch traced here: 203 us
  Pallas kernels  196 us (96%)
  matrix products  2.89 us (1%)
  local copies, waits for them, and re-layouts  2.43 us (1%)
    pallas_call x1, Pallas kernels, fused(): pl.pallas_call(kernel, out_shape=(*[shape((n, rows // n, rank), F32)] * 4...  196 us
  transfers between devices with their start and end apart: 1, of which 1 were waited for; matrix products, arithmetic and copies ran while one was open for 0% of the time, Pallas kernels for 0%

profile of v1, /device:TPU:0, one launch (start us, length us, event | category | flops | bytes accessed | tf_op | source)
XLA Modules:
  0.0 203.5 jit_solution(1760895033722057247)
XLA Ops:
  0.0 0.0 copy-start.3
  0.0 195.9 %shard_map.100 = (f32[8,64,64]{2,1,0:T(8,128)}, f32[8,64,64]{2,1,0:T(8,128)}, f32[8,64,64]{2,1,0:T(8,128)}, f32[8,64,64]{2,1,0:T(8,128)}, bf16[4096,3584]{1,0:T(...) custom-call(bf16[512,1024]{1,0:T(8,128)(2,1)} %tok.1, bf16[512,1024]{1,0:T(8,128)(2,1)} %cot.1, ...), custom_call_target="tpu_custom_call" | custom-call | tf_op jit(solution)/shard_map/pallas_call | solution.py:403
  196.0 0.0 copy-start.2
  196.0 1.1 copy.11
  197.1 1.1 copy.13
  198.1 0.0 copy-done.3
  198.2 0.0 copy-start.1
  198.2 0.3 broadcast_multiply_fusion.1
  198.4 0.0 copy-start
  198.4 0.0 copy-start.4
  198.5 0.0 copy-done.2
  198.5 1.0 fusion.13
  199.5 0.1 reshape.63
  199.6 0.0 copy-done.1
  199.6 1.0 fusion.14
  200.6 0.1 reshape.65
  200.7 0.0 copy-done
  200.7 0.0 copy-done.4
  200.7 0.9 fusion
  201.7 0.1 collective-permute-start
  201.7 1.1 collective-permute-done
  202.9 0.6 dynamic-slice_add_fusion
  (2 shorter events, 0.0 us)
Async XLA Ops:
  0.0 198.1 %copy-start.3 = (s32[512]{0:T(512)S(1)}, s32[512]{0:T(512)}, u32[]{:S(2)}) copy-start(s32[512]{0:T(512)} %param.18) | copy-start | bytes 6148
  196.0 2.5 %copy-start.2 = (f32[8,64,64]{2,1,0:T(8,128)S(1)}, f32[8,64,64]{2,1,0:T(8,128)}, u32[]{:S(2)}) copy-start(f32[8,64,64]{2,1,0:T(8,128)} %get-tuple-element.11) | copy-start | bytes 393220
  198.2 1.4 copy-start.1
  198.4 2.3 %copy-start = (bf16[32,8192]{1,0:T(8,128)(2,1)S(1)}, bf16[32,8192]{1,0:T(8,128)(2,1)}, u32[]{:S(2)}) copy-start(bf16[32,8192]{1,0:T(8,128)(2,1)} %qry.1) | copy-start | bytes 1572868
  198.4 2.3 %copy-start.4 = (bf16[32,8192]{1,0:T(8,128)(2,1)S(1)}, bf16[32,8192]{1,0:T(8,128)(2,1)}, u32[]{:S(2)}) copy-start(bf16[32,8192]{1,0:T(8,128)(2,1)} %get-tuple-element.14) | copy-start | bytes 1572868
  201.7 1.2 collective-permute-start
